TPU v7x, 128 devices: a whole 4x4x4 slice. The times are simulated.
128 devices in a mesh: ctx: 32 (over y, x, z_hi), tp: 4 (over z_lo, core).
Axes of the slice: x: 4, y: 4, z: 4 (z_hi: 2, z_lo: 2; z = z_hi * 2 + z_lo), core: 2. Of those that a mesh axis runs over, the one named last changes fastest.
Arguments:
- tokens: bfloat16 [16384, 4096], P('ctx', 'tp'), may hold values from -48 to 48
- doc_ids: int32 [16384], P('ctx'), may hold values from 0 to 15, never falling along the last dimension, each value on 1 to 8192 neighbouring positions
- w_query: bfloat16 [4096, 2048], P(None, 'tp'), may hold values from -0.09375 to 0.09375
- key_matrix: bfloat16 [4096, 512], P(None, 'tp'), may hold values from -0.09375 to 0.09375
- value_matrix: bfloat16 [4096, 512], P(None, 'tp'), may hold values from -0.09375 to 0.09375
- w_out: bfloat16 [2048, 4096], P('tp'), may hold values from -0.125 to 0.125
Outputs:
- attended: bfloat16 [16384, 4096], P('ctx', 'tp')
Inputs may be any that keep to these rules, and one draw needn't show every extreme that they name: `doc_ids`: document numbers never fall along the rows; one document has exactly 8192 rows.
All inputs are finite; a program needn't handle non-finite values.
Results may differ from a plain program's by a relative error of at most 0.015.
The roundings to bfloat16 on the way count: a program that leaves them out, or rounds other values in their place, can miss the bound.
Values may be sent and summed in bfloat16 or wider, within the bound.
A program may use at most 128 MiB of HBM per device.

v0:
```python
import math

import jax
import jax.numpy as jnp
from jax import lax
from jax.experimental import pallas as pl
from jax.experimental.pallas import tpu as pltpu
from jax.sharding import PartitionSpec as P

MESH = pl.DeviceIdType.MESH
BF, F32 = jnp.bfloat16, jnp.float32
HEAD = 128
GROUP = 4
R = 128
CH = 4
AHEAD = 2
BLK = R * CH
FEAT = 16
BIG = 2.0**50
SCALE = math.log2(math.e) / math.sqrt(HEAD)
KROWS = HEAD + FEAT + HEAD
QROWS = HEAD + FEAT
QCOLS = GROUP * R
QUARTER = 1024


def kernel(
    tok_ref, ids_ref, wq_ref, wk_ref, wv_ref, wo_ref, out_ref,
    tok, wq, wkv, wo, kv, kf, qm, acc, top, osend, lsend, ret, retl, oown, lown,
    sibsend, sibrecv, ownp, matesend, materecv,
    load_sem, tsend, trecv, zsend, zrecv, xsend, xrecv, qsend, qrecv,
    rsend, rrecv, lssend, lsrecv, ssend, srecv, msend, mrecv,
):
    ctx, tp = lax.axis_index("ctx"), lax.axis_index("tp")
    y, p = ctx // 8, ctx % 8
    x, zh = p // 2, p % 2
    zl, co = tp // 2, tp % 2
    sib = (ctx, zl * 2 + 1 - co)
    mate = (ctx, (1 - zl) * 2 + co)
    twin = (y * 8 + x * 2 + 1 - zh, tp)
    xs = [(y * 8 + ((x + d) % 4) * 2 + zh, tp) for d in (1, 2, 3)]
    ys = [(((y + d) % 4) * 8 + p, tp) for d in (1, 2, 3)]
    pt = x * 2 + 1 - zh

    def remote(src, dst, s, r, where):
        return pltpu.make_async_remote_copy(
            src_ref=src, dst_ref=dst, send_sem=s, recv_sem=r, device_id=where, device_id_type=MESH
        )

    def rows(c):
        return pl.ds(pl.multiple_of(c * R, R), R)

    def cols(t):
        return pl.ds(pl.multiple_of(t * QUARTER, QUARTER), QUARTER)

    mine = pltpu.make_async_copy(tok_ref, tok.at[:, cols(tp)], load_sem.at[0])
    mine.start()
    loads = [
        pltpu.make_async_copy(wk_ref, wkv.at[:, pl.ds(0, HEAD)], load_sem.at[1]),
        pltpu.make_async_copy(wv_ref, wkv.at[:, pl.ds(HEAD, HEAD)], load_sem.at[2]),
        pltpu.make_async_copy(wq_ref, wq, load_sem.at[3]),
    ]
    wo_loads = [
        pltpu.make_async_copy(wo_ref.at[:, pl.ds(t * QUARTER, QUARTER)], wo.at[t], load_sem.at[4 + t])
        for t in range(4)
    ]
    for load in loads + wo_loads:
        load.start()

    for c in range(CH):
        acc[2 + c] = jnp.zeros(acc.shape[1:], F32)
        top[2 + c] = jnp.full(top.shape[1:], -1e37, F32)

    barrier = pltpu.get_barrier_semaphore()
    peers = [sib, mate, twin] + xs + ys
    for peer in peers:
        pl.semaphore_signal(barrier, inc=1, device_id=peer, device_id_type=MESH)
    pl.semaphore_wait(barrier, len(peers))
    mine.wait()

    def tok_copy(kind, c):
        t = [tp, tp, (1 - zl) * 2 + co][kind]
        piece = tok.at[rows(c), cols(t)]
        return remote(piece, piece, tsend.at[kind, c], trecv.at[kind, c], [sib, mate, sib][kind])

    for c in range(AHEAD):
        tok_copy(1, c).start()
    for c in range(CH):
        tok_copy(0, c).start()
    for load in loads:
        load.wait()

    def twin_copy(c):
        return remote(kv.at[p, c], kv.at[p, c], zsend.at[c], zrecv.at[c], twin)

    def x_copy(kind, d, c):
        j = [p, pt][kind]
        return remote(kv.at[j, c], kv.at[j, c], xsend.at[kind, d, c], xrecv.at[kind, d, c], xs[d])

    def q_copy(k, c):
        return remote(qm.at[0, c], qm.at[k + 1, c], qsend.at[k, c], qrecv.at[k, c], ys[2 - k])

    def forward(c):
        twin_copy(c).wait_recv()
        for d in range(3):
            x_copy(1, d, c).start()

    def keys_in(c):
        for kind in range(2):
            for d in range(3):
                x_copy(kind, d, c).wait_recv()

        hot = jnp.concatenate([kv[j, c, HEAD : HEAD + FEAT, :] for j in range(8)], axis=0)
        hot = hot.astype(F32).T.astype(BF)
        block = lax.broadcasted_iota(jnp.int32, (R, HEAD), 1) // FEAT
        for j in range(8):
            kf[j, c] = jnp.where(block == j, hot, jnp.zeros_like(hot))

    def pieces(kind, t):
        if kind == "chunk":
            return [(j, t) for j in range(8)]
        return [(2 * t + j, i) for j in range(2) for i in range(CH)]

    def scores(slot, c, kind, t):
        k = jnp.concatenate(
            [jnp.concatenate([kv[j, i, :HEAD, :], kf[j, i]], axis=1) for j, i in pieces(kind, t)],
            axis=0,
        )
        q = jnp.concatenate([qm[slot, c, :HEAD]] + [qm[slot, c, HEAD:]] * 8, axis=0)
        return jnp.dot(k, q, preferred_element_type=F32)

    def add(state, kind, t, s):
        v = jnp.concatenate([kv[j, i, HEAD + FEAT :, :] for j, i in pieces(kind, t)], axis=1)
        v = jnp.concatenate([v, jnp.ones((FEAT, 2 * BLK), BF)], axis=0)
        old = top[state, 0:1, :]
        new = jnp.maximum(old, jnp.max(s, axis=0, keepdims=True))
        w = jnp.exp2((s - new) * SCALE).astype(BF)
        factor = jnp.exp2((old - new) * SCALE)
        acc[state] = acc[state] * factor + jnp.dot(v, w, preferred_element_type=F32)
        top[state, 0:1, :] = new

    def final(state):
        total = acc[state, HEAD : HEAD + 1, :]
        return acc[state, :HEAD, :] / total, top[state, 0:1, :] * SCALE + jnp.log2(total)

    def early(new_queries, pairs):
        @pl.when(y <= 2)
        def _():
            for c in new_queries:
                q_copy(0, c).wait_recv()
            held = None
            for c, t in pairs:
                s = scores(1, c, "chunk", t)
                if held is not None:
                    add(*held)
                held = (2 + c, "chunk", t, s)
            add(*held)

    @pl.loop(0, CH)
    def _(c):
        tok_copy(1, c).wait_recv()
        tok_copy(2, c).start()
        tok_copy(0, c).wait_recv()
        tok_copy(2, c).wait_recv()
        block = tok[rows(c), :]
        kvf = jnp.dot(block, wkv[...], preferred_element_type=F32)
        same = lax.broadcasted_iota(jnp.int32, (FEAT, R), 0) == ids_ref[c]
        kv[p, c, :HEAD, :] = kvf[:, :HEAD].astype(BF)
        kv[p, c, HEAD : HEAD + FEAT, :] = jnp.where(same, BIG, 0.0).astype(BF)
        kv[p, c, HEAD + FEAT :, :] = kvf[:, HEAD:].T.astype(BF)
        twin_copy(c).start()

        @pl.when(c + AHEAD < CH)
        def _():
            tok_copy(1, c + AHEAD).start()

        for d in range(3):
            x_copy(0, d, c).start()
        qf = jnp.dot(block, wq[...], preferred_element_type=F32)
        feat = jnp.where(same, 0.0, -BIG).astype(BF)
        for h in range(GROUP):
            qm[0, c, :HEAD, h * R : (h + 1) * R] = qf[:, h * HEAD : (h + 1) * HEAD].T.astype(BF)
            qm[0, c, HEAD:, h * R : (h + 1) * R] = feat
        for k in range(2):

            @pl.when(y >= k + 1)
            def _():
                q_copy(k, c).start()

        @pl.when(c >= 1)
        def _():
            forward(c - 1)

        @pl.when(c >= 2)
        def _():
            keys_in(c - 2)

        @pl.when(c == 2)
        def _():
            early([0], [(0, 0)])

        @pl.when(c == 3)
        def _():
            early([1], [(0, 1), (1, 0), (1, 1)])

    forward(3)

    for k in range(2):

        @pl.when(y < k + 1)
        def _():
            ret[k] = jnp.zeros(ret.shape[1:], BF)
            retl[k] = jnp.full(retl.shape[1:], -1e30, F32)

    early([2, 3], [(2, 0), (2, 1), (3, 0), (3, 1)])
    keys_in(2)
    early([], [(0, 2), (1, 2), (2, 2), (3, 2)])
    keys_in(3)

    def o_copy(k, c):
        return remote(osend.at[k, c], ret.at[k, c], rsend.at[k, c], rrecv.at[k, c], ys[k])

    def l_copy(k, c):
        return remote(lsend.at[k, c], retl.at[k, c], lssend.at[k, c], lsrecv.at[k, c], ys[k])

    def send_back(k, c):
        o, l = final([2 + c, 1][k])
        osend[k, c] = o.astype(BF)
        lsend[k, c] = jnp.broadcast_to(l, (8, QCOLS))

        @pl.when(y <= 2 - k)
        def _():
            o_copy(k, c).start()
            l_copy(k, c).start()

    def attend(c):
        acc[0:2] = jnp.zeros((2,) + acc.shape[1:], F32)
        top[0:2] = jnp.full((2,) + top.shape[1:], -1e37, F32)

        @pl.when(y <= 1)
        def _():
            q_copy(1, c).wait_recv()

        items = [(2 + c, 1, "chunk", 3), (1, 2, "pair", x)]
        for i in range(3):
            t = (x + 1 + i) % 4
            items.append((jnp.where(t > x, 1, 0), jnp.where(t > x, 2, 0), "pair", t))
        items.append((0, 0, "pair", x))
        held = None
        for i, (state, slot, kind, t) in enumerate(items):
            s = scores(slot, c, kind, t)
            if i == 5:
                key = lax.broadcasted_iota(jnp.int32, (2 * BLK, QCOLS), 0)
                row = zh * BLK + c * R + lax.broadcasted_iota(jnp.int32, (1, QCOLS), 1) % R
                s = jnp.where(key <= row, s, -2e30)
            if held is not None:
                add(*held)
            held = (state, kind, t, s)
            if i == 1:
                send_back(0, c)
            if i == 3:

                @pl.when(c >= 1)
                def _():
                    project(c - 1)

            if i == 5:
                send_back(1, c)

                @pl.when(c >= 1)
                def _():
                    exchange(c - 1)

        add(*held)
        o, l = final(0)
        oown[c] = o
        lown[c] = jnp.broadcast_to(l, (8, QCOLS))

    def sib_copy(c):
        return remote(sibsend.at[c], sibrecv.at[c], ssend.at[c], srecv.at[c], sib)

    def mate_copy(c):
        return remote(matesend.at[c], materecv.at[c], msend.at[c], mrecv.at[c], mate)

    def project(c):
        for k in range(2):

            @pl.when(y >= k + 1)
            def _():
                o_copy(k, c).wait_recv()
                l_copy(k, c).wait_recv()

        ls = [lown[c, 0:1, :], retl[0, c, 0:1, :], retl[1, c, 0:1, :]]
        most = jnp.maximum(jnp.maximum(ls[0], ls[1]), ls[2])
        ws = [jnp.exp2(l - most) for l in ls]
        den = ws[0] + ws[1] + ws[2]
        o = (
            oown[c] * (ws[0] / den)
            + ret[0, c].astype(F32) * (ws[1] / den)
            + ret[1, c].astype(F32) * (ws[2] / den)
        )
        context = jnp.concatenate(
            [o[:, h * R : (h + 1) * R].T.astype(BF) for h in range(GROUP)], axis=1
        )
        for z in range(2):
            chip = (zl + z) % 2
            sibsend[c, z] = jnp.dot(
                context, wo[chip * 2 + 1 - co], preferred_element_type=F32
            ).astype(BF)
        sib_copy(c).start()
        for z in range(2):
            chip = (zl + z) % 2
            ownp[c, z] = jnp.dot(context, wo[chip * 2 + co], preferred_element_type=F32)

    def exchange(c):
        sib_copy(c).wait_recv()
        matesend[c] = (ownp[c, 1] + sibrecv[c, 1].astype(F32)).astype(BF)
        mate_copy(c).start()
        ownp[c, 0] = ownp[c, 0] + sibrecv[c, 0].astype(F32)

    for load in wo_loads:
        load.wait()

    pl.loop(0, CH)(attend)
    project(CH - 1)
    exchange(CH - 1)

    @pl.loop(0, CH)
    def _(c):
        mate_copy(c).wait_recv()
        out_ref[rows(c), :] = (ownp[c, 0] + materecv[c].astype(F32)).astype(BF)

    @pl.loop(0, CH)
    def _(c):
        for kind in range(3):
            tok_copy(kind, c).wait_send()
        twin_copy(c).wait_send()
        for kind in range(2):
            for d in range(3):
                x_copy(kind, d, c).wait_send()
        for k in range(2):

            @pl.when(y >= k + 1)
            def _():
                q_copy(k, c).wait_send()

            @pl.when(y <= 2 - k)
            def _():
                o_copy(k, c).wait_send()
                l_copy(k, c).wait_send()

        sib_copy(c).wait_send()
        mate_copy(c).wait_send()


def on_device(tokens, doc_ids, w_query, key_matrix, value_matrix, w_out):
    width = 4 * QUARTER
    dma = pltpu.SemaphoreType.DMA
    vmem = pltpu.VMEM
    far = pl.BlockSpec(memory_space=pl.ANY)
    near = pl.BlockSpec(memory_space=pltpu.VMEM)
    return pl.pallas_call(
        kernel,
        out_shape=jax.ShapeDtypeStruct((BLK, QUARTER), BF),
        in_specs=[far, near, far, far, far, far],
        out_specs=near,
        scratch_shapes=[
            vmem((BLK, width), BF),
            vmem((width, GROUP * HEAD), BF),
            vmem((width, 2 * HEAD), BF),
            vmem((4, GROUP * HEAD, QUARTER), BF),
            vmem((8, CH, KROWS, R), BF),
            vmem((8, CH, R, HEAD), BF),
            vmem((3, CH, QROWS, QCOLS), BF),
            vmem((2 + CH, HEAD + FEAT, QCOLS), F32),
            vmem((2 + CH, 8, QCOLS), F32),
            vmem((2, CH, HEAD, QCOLS), BF),
            vmem((2, CH, 8, QCOLS), F32),
            vmem((2, CH, HEAD, QCOLS), BF),
            vmem((2, CH, 8, QCOLS), F32),
            vmem((CH, HEAD, QCOLS), F32),
            vmem((CH, 8, QCOLS), F32),
            vmem((CH, 2, R, QUARTER), BF),
            vmem((CH, 2, R, QUARTER), BF),
            vmem((CH, 2, R, QUARTER), F32),
            vmem((CH, R, QUARTER), BF),
            vmem((CH, R, QUARTER), BF),
            dma((8,)),
            dma((3, CH)), dma((3, CH)),
            dma((CH,)), dma((CH,)),
            dma((2, 3, CH)), dma((2, 3, CH)),
            dma((2, CH)), dma((2, CH)),
            dma((2, CH)), dma((2, CH)),
            dma((2, CH)), dma((2, CH)),
            dma((CH,)), dma((CH,)),
            dma((CH,)), dma((CH,)),
        ],
        compiler_params=pltpu.CompilerParams(
            collective_id=0, has_side_effects=True, vmem_limit_bytes=60 * 2**20
        ),
        cost_estimate=pl.CostEstimate(flops=30 * 10**9, bytes_accessed=12 * 2**20, transcendentals=0),
        name="attention",
    )(tokens, doc_ids.reshape(CH, 1, R), w_query, key_matrix, value_matrix, w_out)


def solution(mesh):
    placed = (P("ctx", "tp"), P("ctx"), P(None, "tp"), P(None, "tp"), P(None, "tp"), P("tp", None))
    return jax.shard_map(
        on_device, mesh=mesh, in_specs=placed, out_specs=P("ctx", "tp"), check_vma=False
    )
```

profile of v0, /device:TPU:49, one launch (start us, length us, event | category | flops | bytes accessed | tf_op | source)
XLA Modules:
  0.0 88.8 jit_solution(3419079206015945625)
XLA Ops:
  0.0 86.5 %attention.1 = bf16[512,1024]{1,0:T(8,128)(2,1)} custom-call(bf16[512,1024]{1,0:T(8,128)(2,1)} %tok_ref.1, s32[4,1,128]{2,1,0:T(1,128)} %bitcast.1, bf16[4096,512]{1,0:T(8,128)(2,1)} %wq_ref.1, bf16[4096,128]{1,0:T(8,128)(2,1)} %wk_ref.1, bf16[4096,128]{1,0:T(8,128)(2,1)} %wv_ref.1, bf16[512,4096]{1,0:T(8,128)(2,1)} %wo_ref.1), custom_call_target="tpu_custom_call" | custom-call | flops 30000001024 | bytes 12582912 | tf_op jit(solution)/shard_map/attention/pallas_call | solution.py:362
  86.5 2.3 %copy.8 = bf16[512,1024]{1,0:T(8,128)(2,1)} copy(bf16[512,1024]{1,0:T(8,128)(2,1)} %attention.1) | data formatting | bytes 2097152
where the time goes:
time: 89.5 us; the launch traced here: 88.8 us
  Pallas kernels  86.5 us (97%)
  local copies, waits for them, and re-layouts  2.26 us (3%)
    pallas_call x1, Pallas kernels, on_device(): pl.pallas_call(kernel, out_shape=jax.ShapeDtypeStruct((BLK, QUARTER), BF)...  86.5 us
    unnamed x1, local copies, waits for them, and re-layouts  2.26 us

commit v1 on v0

--- a/solution.py
+++ b/solution.py
@@ -27,9 +27,9 @@
 def kernel(
     tok_ref, ids_ref, wq_ref, wk_ref, wv_ref, wo_ref, out_ref,
     tok, wq, wkv, wo, kv, kf, qm, acc, top, osend, lsend, ret, retl, oown, lown,
-    sibsend, sibrecv, ownp, matesend, materecv,
+    context,
     load_sem, tsend, trecv, zsend, zrecv, xsend, xrecv, qsend, qrecv,
-    rsend, rrecv, lssend, lsrecv, ssend, srecv, msend, mrecv,
+    rsend, rrecv, lssend, lsrecv, csend, crecv, wsend, wrecv,
 ):
     ctx, tp = lax.axis_index("ctx"), lax.axis_index("tp")
     y, p = ctx // 8, ctx % 8
@@ -41,6 +41,8 @@
     xs = [(y * 8 + ((x + d) % 4) * 2 + zh, tp) for d in (1, 2, 3)]
     ys = [(((y + d) % 4) * 8 + p, tp) for d in (1, 2, 3)]
     pt = x * 2 + 1 - zh
+    behind = y * 8 + pt
+    others = [sib, (behind, (1 - zl) * 2 + co), (behind, (1 - zl) * 2 + 1 - co)]
 
     def remote(src, dst, s, r, where):
         return pltpu.make_async_remote_copy(
@@ -49,6 +51,9 @@
 
     def rows(c):
         return pl.ds(pl.multiple_of(c * R, R), R)
+
+    def heads(t):
+        return pl.ds(pl.multiple_of(t * GROUP * HEAD, GROUP * HEAD), GROUP * HEAD)
 
     def cols(t):
         return pl.ds(pl.multiple_of(t * QUARTER, QUARTER), QUARTER)
@@ -60,11 +65,8 @@
         pltpu.make_async_copy(wv_ref, wkv.at[:, pl.ds(HEAD, HEAD)], load_sem.at[2]),
         pltpu.make_async_copy(wq_ref, wq, load_sem.at[3]),
     ]
-    wo_loads = [
-        pltpu.make_async_copy(wo_ref.at[:, pl.ds(t * QUARTER, QUARTER)], wo.at[t], load_sem.at[4 + t])
-        for t in range(4)
-    ]
-    for load in loads + wo_loads:
+    loads_wo = pltpu.make_async_copy(wo_ref.at[:, cols(tp)], wo.at[heads(tp), :], load_sem.at[4])
+    for load in loads + [loads_wo]:
         load.start()
 
     for c in range(CH):
@@ -72,7 +74,7 @@
         top[2 + c] = jnp.full(top.shape[1:], -1e37, F32)
 
     barrier = pltpu.get_barrier_semaphore()
-    peers = [sib, mate, twin] + xs + ys
+    peers = [mate, twin] + others + xs + ys
     for peer in peers:
         pl.semaphore_signal(barrier, inc=1, device_id=peer, device_id_type=MESH)
     pl.semaphore_wait(barrier, len(peers))
@@ -87,6 +89,13 @@
         tok_copy(1, c).start()
     for c in range(CH):
         tok_copy(0, c).start()
+    def wo_copy(i):
+        return remote(
+            wo_ref.at[:, cols(others[i][1])], wo.at[heads(tp), :], wsend.at[i], wrecv.at[i], others[i]
+        )
+
+    for i in range(3):
+        wo_copy(i).start()
     for load in loads:
         load.wait()
 
@@ -160,6 +169,11 @@
     def _(c):
         tok_copy(1, c).wait_recv()
         tok_copy(2, c).start()
+
+        @pl.when(c >= 1)
+        def _():
+            forward(c - 1)
+
         tok_copy(0, c).wait_recv()
         tok_copy(2, c).wait_recv()
         block = tok[rows(c), :]
@@ -181,15 +195,14 @@
         for h in range(GROUP):
             qm[0, c, :HEAD, h * R : (h + 1) * R] = qf[:, h * HEAD : (h + 1) * HEAD].T.astype(BF)
             qm[0, c, HEAD:, h * R : (h + 1) * R] = feat
-        for k in range(2):
-
-            @pl.when(y >= k + 1)
-            def _():
-                q_copy(k, c).start()
-
-        @pl.when(c >= 1)
-        def _():
-            forward(c - 1)
+
+        @pl.when(y >= 1)
+        def _():
+            q_copy(0, c).start()
+
+        @pl.when((c >= 1) & (y >= 2))
+        def _():
+            q_copy(1, c - 1).start()
 
         @pl.when(c >= 2)
         def _():
@@ -197,11 +210,11 @@
 
         @pl.when(c == 2)
         def _():
-            early([0], [(0, 0)])
+            early([0, 1], [(0, 0), (1, 0)])
 
         @pl.when(c == 3)
         def _():
-            early([1], [(0, 1), (1, 0), (1, 1)])
+            early([2], [(0, 1), (1, 1), (2, 0), (2, 1)])
 
     forward(3)
 
@@ -212,9 +225,13 @@
             ret[k] = jnp.zeros(ret.shape[1:], BF)
             retl[k] = jnp.full(retl.shape[1:], -1e30, F32)
 
-    early([2, 3], [(2, 0), (2, 1), (3, 0), (3, 1)])
+    @pl.when(y >= 2)
+    def _():
+        q_copy(1, CH - 1).start()
+
     keys_in(2)
-    early([], [(0, 2), (1, 2), (2, 2), (3, 2)])
+    early([], [(0, 2), (1, 2), (2, 2)])
+    early([3], [(3, 0), (3, 1), (3, 2)])
     keys_in(3)
 
     def o_copy(k, c):
@@ -241,7 +258,7 @@
         def _():
             q_copy(1, c).wait_recv()
 
-        items = [(2 + c, 1, "chunk", 3), (1, 2, "pair", x)]
+        items = [(1, 2, "pair", x)]
         for i in range(3):
             t = (x + 1 + i) % 4
             items.append((jnp.where(t > x, 1, 0), jnp.where(t > x, 2, 0), "pair", t))
@@ -249,40 +266,40 @@
         held = None
         for i, (state, slot, kind, t) in enumerate(items):
             s = scores(slot, c, kind, t)
-            if i == 5:
+            if i == 4:
                 key = lax.broadcasted_iota(jnp.int32, (2 * BLK, QCOLS), 0)
                 row = zh * BLK + c * R + lax.broadcasted_iota(jnp.int32, (1, QCOLS), 1) % R
                 s = jnp.where(key <= row, s, -2e30)
             if held is not None:
                 add(*held)
             held = (state, kind, t, s)
-            if i == 1:
-                send_back(0, c)
-            if i == 3:
-
-                @pl.when(c >= 1)
+            if i == 4:
+                send_back(1, c)
+
+                @pl.when(c + 1 < CH)
                 def _():
-                    project(c - 1)
-
-            if i == 5:
-                send_back(1, c)
-
-                @pl.when(c >= 1)
-                def _():
-                    exchange(c - 1)
+                    send_back(0, c + 1)
+
 
         add(*held)
         o, l = final(0)
         oown[c] = o
         lown[c] = jnp.broadcast_to(l, (8, QCOLS))
 
-    def sib_copy(c):
-        return remote(sibsend.at[c], sibrecv.at[c], ssend.at[c], srecv.at[c], sib)
-
-    def mate_copy(c):
-        return remote(matesend.at[c], materecv.at[c], msend.at[c], mrecv.at[c], mate)
-
-    def project(c):
+        @pl.when(c >= 1)
+        def _():
+            merge(c - 1)
+
+        @pl.when(c >= 2)
+        def _():
+            relay(c - 2)
+
+    def context_copy(kind, c):
+        t = [tp, tp, (1 - zl) * 2 + co][kind]
+        piece = context.at[t, c]
+        return remote(piece, piece, csend.at[kind, c], crecv.at[kind, c], [sib, mate, sib][kind])
+
+    def merge(c):
         for k in range(2):
 
             @pl.when(y >= k + 1)
@@ -299,36 +316,30 @@
             + ret[0, c].astype(F32) * (ws[1] / den)
             + ret[1, c].astype(F32) * (ws[2] / den)
         )
-        context = jnp.concatenate(
+        context[tp, c] = jnp.concatenate(
             [o[:, h * R : (h + 1) * R].T.astype(BF) for h in range(GROUP)], axis=1
         )
-        for z in range(2):
-            chip = (zl + z) % 2
-            sibsend[c, z] = jnp.dot(
-                context, wo[chip * 2 + 1 - co], preferred_element_type=F32
-            ).astype(BF)
-        sib_copy(c).start()
-        for z in range(2):
-            chip = (zl + z) % 2
-            ownp[c, z] = jnp.dot(context, wo[chip * 2 + co], preferred_element_type=F32)
-
-    def exchange(c):
-        sib_copy(c).wait_recv()
-        matesend[c] = (ownp[c, 1] + sibrecv[c, 1].astype(F32)).astype(BF)
-        mate_copy(c).start()
-        ownp[c, 0] = ownp[c, 0] + sibrecv[c, 0].astype(F32)
-
-    for load in wo_loads:
-        load.wait()
-
+        context_copy(1, c).start()
+        context_copy(0, c).start()
+
+    def relay(c):
+        context_copy(1, c).wait_recv()
+        context_copy(2, c).start()
+
+    def output(c):
+        context_copy(0, c).wait_recv()
+        context_copy(2, c).wait_recv()
+        whole = jnp.concatenate([context[t, c] for t in range(4)], axis=1)
+        out_ref[rows(c), :] = jnp.dot(whole, wo[...], preferred_element_type=F32).astype(BF)
+
+    early([], [(0, 3), (1, 3), (2, 3), (3, 3)])
+    send_back(0, 0)
     pl.loop(0, CH)(attend)
-    project(CH - 1)
-    exchange(CH - 1)
-
-    @pl.loop(0, CH)
-    def _(c):
-        mate_copy(c).wait_recv()
-        out_ref[rows(c), :] = (ownp[c, 0] + materecv[c].astype(F32)).astype(BF)
+    loads_wo.wait()
+    for i in range(3):
+        wo_copy(i).wait_recv()
+    output(CH - 4)
+    output(CH - 3)
 
     @pl.loop(0, CH)
     def _(c):
@@ -344,13 +355,23 @@
             def _():
                 q_copy(k, c).wait_send()
 
+    for i in range(3):
+        wo_copy(i).wait_send()
+    merge(CH - 1)
+    relay(CH - 2)
+    output(CH - 2)
+    relay(CH - 1)
+    output(CH - 1)
+
+    for c in range(CH):
+        for kind in range(3):
+            context_copy(kind, c).wait_send()
+        for k in range(2):
+
             @pl.when(y <= 2 - k)
             def _():
                 o_copy(k, c).wait_send()
                 l_copy(k, c).wait_send()
-
-        sib_copy(c).wait_send()
-        mate_copy(c).wait_send()
 
 
 def on_device(tokens, doc_ids, w_query, key_matrix, value_matrix, w_out):
@@ -361,14 +382,14 @@
     near = pl.BlockSpec(memory_space=pltpu.VMEM)
     return pl.pallas_call(
         kernel,
-        out_shape=jax.ShapeDtypeStruct((BLK, QUARTER), BF),
+        out_shape=pltpu.VMEM((BLK, QUARTER), BF),
         in_specs=[far, near, far, far, far, far],
         out_specs=near,
         scratch_shapes=[
             vmem((BLK, width), BF),
             vmem((width, GROUP * HEAD), BF),
             vmem((width, 2 * HEAD), BF),
-            vmem((4, GROUP * HEAD, QUARTER), BF),
+            vmem((4 * GROUP * HEAD, QUARTER), BF),
             vmem((8, CH, KROWS, R), BF),
             vmem((8, CH, R, HEAD), BF),
             vmem((3, CH, QROWS, QCOLS), BF),
@@ -380,20 +401,16 @@
             vmem((2, CH, 8, QCOLS), F32),
             vmem((CH, HEAD, QCOLS), F32),
             vmem((CH, 8, QCOLS), F32),
-            vmem((CH, 2, R, QUARTER), BF),
-            vmem((CH, 2, R, QUARTER), BF),
-            vmem((CH, 2, R, QUARTER), F32),
-            vmem((CH, R, QUARTER), BF),
-            vmem((CH, R, QUARTER), BF),
-            dma((8,)),
+            vmem((4, CH, R, GROUP * HEAD), BF),
+            dma((5,)),
             dma((3, CH)), dma((3, CH)),
             dma((CH,)), dma((CH,)),
             dma((2, 3, CH)), dma((2, 3, CH)),
             dma((2, CH)), dma((2, CH)),
             dma((2, CH)), dma((2, CH)),
             dma((2, CH)), dma((2, CH)),
-            dma((CH,)), dma((CH,)),
-            dma((CH,)), dma((CH,)),
+            dma((3, CH)), dma((3, CH)),
+            dma((3,)), dma((3,)),
         ],
         compiler_params=pltpu.CompilerParams(
             collective_id=0, has_side_effects=True, vmem_limit_bytes=60 * 2**20

time: 89.5 us -> 85.8 us (0.959)
  Pallas kernels: 86.5 us -> 84.7 us
  local copies, waits for them, and re-layouts: 2.26 us -> 0.97 us
    pallas_call x1, Pallas kernels: 86.5 us -> 84.7 us  [on_device(): pl.pallas_call(kernel, out_shape=pltpu.VMEM((BLK, QUARTER), BF), in_specs...]
    unnamed x1, local copies, waits for them, and re-layouts: 2.26 us -> 0.97 us
where the time goes in v1:
time: 85.8 us; the launch traced here: 85.6 us
  Pallas kernels  84.7 us (99%)
  local copies, waits for them, and re-layouts  0.97 us (1%)
    pallas_call x1, Pallas kernels, on_device(): pl.pallas_call(kernel, out_shape=pltpu.VMEM((BLK, QUARTER), BF), in_specs...  84.7 us

profile of v1, /device:TPU:49, one launch (start us, length us, event | category | flops | bytes accessed | tf_op | source)
XLA Modules:
  0.0 85.6 jit_solution(4277651996025030239)
XLA Ops:
  0.0 84.7 %attention.1 = bf16[512,1024]{1,0:T(8,128)(2,1)S(1)} custom-call(bf16[512,1024]{1,0:T(8,128)(2,1)} %tok_ref.1, s32[4,1,128]{2,1,0:T(1,128)} %bitcast.1, bf16[4096,512]{1,0:T(8,128)(2,1)} %wq_ref.1, bf16[4096,128]{1,0:T(8,128)(2,1)} %wk_ref.1, bf16[4096,128]{1,0:T(8,128)(2,1)} %wv_ref.1, bf16[512,4096]{1,0:T(8,128)(2,1)} %wo_ref.1), custom_call_target="tpu_custom_call" | custom-call | flops 30000001024 | bytes 12582912 | tf_op jit(solution)/shard_map/attention/pallas_call | solution.py:383
  84.7 1.0 %copy.8 = bf16[512,1024]{1,0:T(8,128)(2,1)} copy(bf16[512,1024]{1,0:T(8,128)(2,1)S(1)} %attention.1) | data formatting | bytes 2097152

commit v2 on v1

--- a/solution.py
+++ b/solution.py
@@ -58,6 +58,11 @@
     def cols(t):
         return pl.ds(pl.multiple_of(t * QUARTER, QUARTER), QUARTER)
 
+    barrier = pltpu.get_barrier_semaphore()
+    peers = [mate, twin] + others + xs + ys
+    for peer in peers:
+        pl.semaphore_signal(barrier, inc=1, device_id=peer, device_id_type=MESH)
+
     mine = pltpu.make_async_copy(tok_ref, tok.at[:, cols(tp)], load_sem.at[0])
     mine.start()
     loads = [
@@ -69,14 +74,6 @@
     for load in loads + [loads_wo]:
         load.start()
 
-    for c in range(CH):
-        acc[2 + c] = jnp.zeros(acc.shape[1:], F32)
-        top[2 + c] = jnp.full(top.shape[1:], -1e37, F32)
-
-    barrier = pltpu.get_barrier_semaphore()
-    peers = [mate, twin] + others + xs + ys
-    for peer in peers:
-        pl.semaphore_signal(barrier, inc=1, device_id=peer, device_id_type=MESH)
     pl.semaphore_wait(barrier, len(peers))
     mine.wait()
 
@@ -96,6 +93,17 @@
 
     for i in range(3):
         wo_copy(i).start()
+    for c in range(CH):
+        acc[2 + c] = jnp.zeros(acc.shape[1:], F32)
+        top[2 + c] = jnp.full(top.shape[1:], -1e37, F32)
+
+    for k in range(2):
+
+        @pl.when(y < k + 1)
+        def _():
+            ret[k] = jnp.zeros(ret.shape[1:], BF)
+            retl[k] = jnp.full(retl.shape[1:], -1e30, F32)
+
     for load in loads:
         load.wait()
 
@@ -218,13 +226,6 @@
 
     forward(3)
 
-    for k in range(2):
-
-        @pl.when(y < k + 1)
-        def _():
-            ret[k] = jnp.zeros(ret.shape[1:], BF)
-            retl[k] = jnp.full(retl.shape[1:], -1e30, F32)
-
     @pl.when(y >= 2)
     def _():
         q_copy(1, CH - 1).start()
@@ -243,7 +244,7 @@
     def send_back(k, c):
         o, l = final([2 + c, 1][k])
         osend[k, c] = o.astype(BF)
-        lsend[k, c] = jnp.broadcast_to(l, (8, QCOLS))
+        lsend[k, c] = l
 
         @pl.when(y <= 2 - k)
         def _():
@@ -276,9 +277,16 @@
             if i == 4:
                 send_back(1, c)
 
-                @pl.when(c + 1 < CH)
+                @pl.when(c + 2 < CH)
                 def _():
-                    send_back(0, c + 1)
+                    send_back(0, c + 2)
+
+                @pl.when(c >= 3)
+                def _():
+                    loads_wo.wait()
+                    for w in range(3):
+                        wo_copy(w).wait_recv()
+                    output(c - 3)
 
 
         add(*held)
@@ -307,7 +315,7 @@
                 o_copy(k, c).wait_recv()
                 l_copy(k, c).wait_recv()
 
-        ls = [lown[c, 0:1, :], retl[0, c, 0:1, :], retl[1, c, 0:1, :]]
+        ls = [lown[c, 0:1, :], retl[0, c], retl[1, c]]
         most = jnp.maximum(jnp.maximum(ls[0], ls[1]), ls[2])
         ws = [jnp.exp2(l - most) for l in ls]
         den = ws[0] + ws[1] + ws[2]
@@ -332,15 +340,11 @@
         whole = jnp.concatenate([context[t, c] for t in range(4)], axis=1)
         out_ref[rows(c), :] = jnp.dot(whole, wo[...], preferred_element_type=F32).astype(BF)
 
-    early([], [(0, 3), (1, 3), (2, 3), (3, 3)])
+    early([], [(0, 3), (1, 3)])
     send_back(0, 0)
+    send_back(0, 1)
+    early([], [(2, 3), (3, 3)])
     pl.loop(0, CH)(attend)
-    loads_wo.wait()
-    for i in range(3):
-        wo_copy(i).wait_recv()
-    output(CH - 4)
-    output(CH - 3)
-
     @pl.loop(0, CH)
     def _(c):
         for kind in range(3):
@@ -357,21 +361,27 @@
 
     for i in range(3):
         wo_copy(i).wait_send()
-    merge(CH - 1)
-    relay(CH - 2)
-    output(CH - 2)
-    relay(CH - 1)
-    output(CH - 1)
-
-    for c in range(CH):
-        for kind in range(3):
-            context_copy(kind, c).wait_send()
+
+    def sent(c):
         for k in range(2):
 
             @pl.when(y <= 2 - k)
             def _():
                 o_copy(k, c).wait_send()
                 l_copy(k, c).wait_send()
+
+        for kind in range(3):
+            context_copy(kind, c).wait_send()
+
+    merge(CH - 1)
+    relay(CH - 2)
+    output(CH - 3)
+    output(CH - 2)
+    for c in range(CH - 1):
+        sent(c)
+    relay(CH - 1)
+    output(CH - 1)
+    sent(CH - 1)
 
 
 def on_device(tokens, doc_ids, w_query, key_matrix, value_matrix, w_out):
@@ -396,9 +406,9 @@
             vmem((2 + CH, HEAD + FEAT, QCOLS), F32),
             vmem((2 + CH, 8, QCOLS), F32),
             vmem((2, CH, HEAD, QCOLS), BF),
-            vmem((2, CH, 8, QCOLS), F32),
+            vmem((2, CH, 1, QCOLS), F32),
             vmem((2, CH, HEAD, QCOLS), BF),
-            vmem((2, CH, 8, QCOLS), F32),
+            vmem((2, CH, 1, QCOLS), F32),
             vmem((CH, HEAD, QCOLS), F32),
             vmem((CH, 8, QCOLS), F32),
             vmem((4, CH, R, GROUP * HEAD), BF),

time: 85.8 us -> 82.1 us (0.957)
  Pallas kernels: 84.7 us -> 81 us
    pallas_call x1, Pallas kernels: 84.7 us -> 81 us  [on_device(): pl.pallas_call(kernel, out_shape=pltpu.VMEM((BLK, QUARTER), BF), in_specs...]
where the time goes in v2:
time: 82.1 us; the launch traced here: 82 us
  Pallas kernels  81 us (99%)
  local copies, waits for them, and re-layouts  0.97 us (1%)
    pallas_call x1, Pallas kernels, on_device(): pl.pallas_call(kernel, out_shape=pltpu.VMEM((BLK, QUARTER), BF), in_specs...  81 us

profile of v2, /device:TPU:49, one launch (start us, length us, event | category | flops | bytes accessed | tf_op | source)
XLA Modules:
  0.0 82.0 jit_solution(1333204504645695251)
XLA Ops:
  0.0 81.0 %attention.1 = bf16[512,1024]{1,0:T(8,128)(2,1)S(1)} custom-call(bf16[512,1024]{1,0:T(8,128)(2,1)} %tok_ref.1, s32[4,1,128]{2,1,0:T(1,128)} %bitcast.1, bf16[4096,512]{1,0:T(8,128)(2,1)} %wq_ref.1, bf16[4096,128]{1,0:T(8,128)(2,1)} %wk_ref.1, bf16[4096,128]{1,0:T(8,128)(2,1)} %wv_ref.1, bf16[512,4096]{1,0:T(8,128)(2,1)} %wo_ref.1), custom_call_target="tpu_custom_call" | custom-call | flops 30000001024 | bytes 12582912 | tf_op jit(solution)/shard_map/attention/pallas_call | solution.py:393
  81.0 1.0 %copy.8 = bf16[512,1024]{1,0:T(8,128)(2,1)} copy(bf16[512,1024]{1,0:T(8,128)(2,1)S(1)} %attention.1) | data formatting | bytes 2097152

commit v3 on v2

--- a/solution.py
+++ b/solution.py
@@ -294,13 +294,13 @@
         oown[c] = o
         lown[c] = jnp.broadcast_to(l, (8, QCOLS))
 
-        @pl.when(c >= 1)
-        def _():
-            merge(c - 1)
-
-        @pl.when(c >= 2)
-        def _():
-            relay(c - 2)
+        @pl.when((y <= 1) | (c >= 1))
+        def _():
+            merge(c - jnp.where(y <= 1, 0, 1))
+
+        @pl.when((c >= 2) | ((y <= 1) & (c >= 1)))
+        def _():
+            relay(c - jnp.where(y <= 1, 1, 2))
 
     def context_copy(kind, c):
         t = [tp, tp, (1 - zl) * 2 + co][kind]
@@ -373,8 +373,11 @@
         for kind in range(3):
             context_copy(kind, c).wait_send()
 
-    merge(CH - 1)
-    relay(CH - 2)
+    @pl.when(y >= 2)
+    def _():
+        merge(CH - 1)
+        relay(CH - 2)
+
     output(CH - 3)
     output(CH - 2)
     for c in range(CH - 1):

time: 82.1 us -> 82.1 us (level)
  no operation moved by 1% of the time
where the time goes in v3:
time: 82.1 us; the launch traced here: 82 us
  Pallas kernels  81 us (99%)
  local copies, waits for them, and re-layouts  0.97 us (1%)
    pallas_call x1, Pallas kernels, on_device(): pl.pallas_call(kernel, out_shape=pltpu.VMEM((BLK, QUARTER), BF), in_specs...  81 us

profile of v3, /device:TPU:49, one launch (start us, length us, event | category | flops | bytes accessed | tf_op | source)
XLA Modules:
  0.0 82.0 jit_solution(13088101614082035693)
XLA Ops:
  0.0 81.0 %attention.1 = bf16[512,1024]{1,0:T(8,128)(2,1)S(1)} custom-call(bf16[512,1024]{1,0:T(8,128)(2,1)} %tok_ref.1, s32[4,1,128]{2,1,0:T(1,128)} %bitcast.1, bf16[4096,512]{1,0:T(8,128)(2,1)} %wq_ref.1, bf16[4096,128]{1,0:T(8,128)(2,1)} %wk_ref.1, bf16[4096,128]{1,0:T(8,128)(2,1)} %wv_ref.1, bf16[512,4096]{1,0:T(8,128)(2,1)} %wo_ref.1), custom_call_target="tpu_custom_call" | custom-call | flops 30000001024 | bytes 12582912 | tf_op jit(solution)/shard_map/attention/pallas_call | solution.py:396
  81.0 1.0 %copy.8 = bf16[512,1024]{1,0:T(8,128)(2,1)} copy(bf16[512,1024]{1,0:T(8,128)(2,1)S(1)} %attention.1) | data formatting | bytes 2097152
